TPU v7x, 512 devices: a whole 4x8x8 slice. The times are simulated.
512 devices in a mesh: hist: 128 (over z, y, core), col: 4 (over x).
Axes of the slice: x: 4, y: 8, z: 8, core: 2. Of those that a mesh axis runs over, the one named last changes fastest.
Arguments:
- sigma_ret: bfloat16 [4, 512, 64, 128], P(None, 'hist', 'col'), may hold values from -6 to 6
- sigma_less: bfloat16 [4, 512, 64, 128], P(None, 'hist', 'col'), may hold values from -6 to 6
- green_less: bfloat16 [512, 96, 64, 128], P('hist', 'col'), may hold values from -0.0234375 to 0.0234375
- green_adv: bfloat16 [512, 96, 64, 128], P('hist', 'col'), may hold values from -0.0234375 to 0.0234375
- time_now: int32 [4], replicated, may hold values from 256 to 511, as said below
- col_start: int32 [96], P('col'), may hold values from 0 to 255
Outputs:
- collision: bfloat16 [4, 96, 64, 128], P(None, 'col')
Inputs may be any that keep to these rules, and one draw needn't show every extreme that they name: Some time row has time_now = 511.
All inputs are finite; a program needn't handle non-finite values.
Results may differ from a plain program's by a relative error of at most 0.001.
Values may be sent and summed in bfloat16 or wider, within the bound.
A program may use at most 64 MiB of HBM per device.

v0:
```python
import jax
import jax.numpy as jnp
from jax import lax
from jax.sharding import PartitionSpec as P


def widen(green, norb):
    real_part = green[..., :norb]
    imag_part = green[..., norb:]
    lower = jnp.concatenate([-imag_part, real_part], axis=-1)
    return jnp.concatenate([green, lower], axis=-2)


def on_device(sigma_ret, sigma_less, green_less, green_adv, time_now, col_start):
    norb = green_less.shape[2]
    tb_local = green_less.shape[0]
    full_ret, full_less = (
        lax.all_gather(sigma_ret, "col", axis=2, tiled=True),
        lax.all_gather(sigma_less, "col", axis=2, tiled=True),
    )
    tbar = lax.axis_index("hist") * tb_local + jnp.arange(tb_local, dtype=jnp.int32)
    zero = jnp.zeros((), green_less.dtype)
    before = (tbar[None, :] <= time_now[:, None])[:, :, None, None]
    full_ret = jnp.where(before, full_ret, zero)
    full_less = jnp.where(before, full_less, zero)
    after = (tbar[:, None] >= col_start[None, :])[:, :, None, None]
    b_less = jnp.where(after, widen(green_less, norb), zero)
    b_adv = jnp.where(after, widen(green_adv, norb), zero)
    term = jnp.einsum("tbik,bckn->tcin", full_ret, b_less, preferred_element_type=jnp.float32)
    term = term + jnp.einsum(
        "tbik,bckn->tcin", full_less, b_adv, preferred_element_type=jnp.float32
    )
    total = lax.psum(term, "hist")
    return total.astype(jnp.bfloat16)


def solution(mesh):
    return jax.shard_map(
        on_device,
        mesh=mesh,
        in_specs=(
            P(None, "hist", "col", None),
            P(None, "hist", "col", None),
            P("hist", "col", None, None),
            P("hist", "col", None, None),
            P(),
            P("col"),
        ),
        out_specs=P(None, "col", None, None),
        check_vma=False,
    )
```

profile of v0, /device:TPU:1, one launch (start us, length us, event | category | flops | bytes accessed | tf_op | source)
XLA Modules:
  0.0 565.7 jit_solution(4808582537118767516)
XLA Ops:
  0.0 0.0 copy-start.1
  0.0 0.0 copy-start
  0.0 0.0 copy-start.4
  0.0 7.0 %slice_negate_fusion = (bf16[4,24,64,64]{3,2,1,0:T(8,128)(2,1)}, bf16[4,24,64,64]{3,2,1,0:T(8,128)(2,1)}, bf16[4,24,64,64]{3,2,1,0:T(8,128)(2,1)}, bf16[4,24,64,64]{3,2,1,0:T(8,128)(2,1)}) fusion(bf16[4,24,64,128]{3,2,1,0:T(8,128)(2,1)} %param.9, bf16[4,24,64,128]{3,2,1,0:T(8,128)(2,1)} %param.8), kind=kLoop, calls=%fused_computation.10 | loop fusion | flops 786432 | bytes 6291456 | tf_op jit(solution)/shard_map/neg | solution.py:10
  7.0 0.0 copy-done.4
  7.0 0.1 broadcast_compare_fusion.1
  7.1 0.0 copy-done.1
  7.1 0.0 copy-done
  7.1 0.0 copy-start.5
  7.1 0.0 copy-start.2
  7.1 5.4 fusion
  12.4 0.0 copy-done.5
  12.5 0.1 broadcast_compare_fusion
  12.5 0.0 copy-done.2
  12.5 10.5 %all_gather.7 = bf16[4,4,64,128]{3,2,1,0:T(8,128)(2,1)S(1)} all-gather(bf16[4,4,16,128]{3,2,1,0:T(8,128)(2,1)S(1)} %copy-done.2), channel_id=1, replica_groups=mesh['hist'=128,'col'=4] {'col'}, dimensions={2}, use_global_device_ids=true | all-gather | bytes 327680 | tf_op jit(solution)/shard_map/all_gather | solution.py:19
  23.1 0.0 copy-start.3
  23.1 1.0 fusion.3
  24.1 0.0 copy-done.3
  24.1 9.4 %all_gather.6 = bf16[4,4,64,128]{3,2,1,0:T(8,128)(2,1)S(1)} all-gather(bf16[4,4,16,128]{3,2,1,0:T(8,128)(2,1)S(1)} %copy-done.3), channel_id=1, replica_groups=mesh['hist'=128,'col'=4] {'col'}, dimensions={2}, use_global_device_ids=true | all-gather | bytes 327680 | tf_op jit(solution)/shard_map/all_gather | solution.py:18
  33.5 1.1 fusion.2
  34.6 528.4 %all-reduce.1 = bf16[4,24,64,128]{3,2,0,1:T(8,128)(2,1)} all-reduce(f32[4,24,64,128]{3,2,0,1:T(8,128)S(1)} %fusion.2), channel_id=1, replica_groups=mesh['hist'=128,'col'=4] {'hist'}, use_global_device_ids=true, to_apply=%region_0.1 | all-reduce | flops 786432 | bytes 4718592 | tf_op jit(solution)/shard_map/psum | solution.py:33
  563.0 2.7 copy.9
  (1 shorter events, 0.0 us)
Async XLA Ops:
  0.0 7.1 %copy-start.1 = (bf16[4,24,64,128]{3,2,1,0:T(8,128)(2,1)S(1)}, bf16[4,24,64,128]{3,2,1,0:T(8,128)(2,1)}, u32[]{:S(2)}) copy-start(bf16[4,24,64,128]{3,2,1,0:T(8,128)(2,1)} %param.8) | copy-start | bytes 4718596
  0.0 7.1 %copy-start = (bf16[4,24,64,128]{3,2,1,0:T(8,128)(2,1)S(1)}, bf16[4,24,64,128]{3,2,1,0:T(8,128)(2,1)}, u32[]{:S(2)}) copy-start(bf16[4,24,64,128]{3,2,1,0:T(8,128)(2,1)} %param.9) | copy-start | bytes 4718596
  0.0 7.0 %copy-start.4 = (s32[24]{0:T(128)S(1)}, s32[24]{0:T(128)}, u32[]{:S(2)}) copy-start(s32[24]{0:T(128)} %param.11) | copy-start | bytes 292
  7.1 5.4 copy-start.5
  7.1 5.5 copy-start.2
  23.1 1.0 copy-start.3
where the time goes:
time: 570 us; the launch traced here: 566 us
  blocking collectives  548 us (96%)
  other arithmetic  12.5 us (2%)
    psum x1, blocking collectives, on_device(): total = lax.psum(term, 'hist')  528 us

commit v1 on v0

v1 whole, which is shorter than its diff:
```python
import functools

import jax
import jax.numpy as jnp
from jax import lax
from jax.experimental import pallas as pl
from jax.experimental.pallas import tpu as pltpu
from jax.sharding import PartitionSpec as P

MESH = pl.DeviceIdType.MESH
RING = 8
COLS = 12
STEP = (0, 1, 3, 2)


def kernel(time_ref, start_ref, sr_ref, sl_ref, gl_ref, ga_ref, out_ref,
           raw, left, green, c_send, c_recv, part, coded, scale, rx_p, rx_q, sc_p, sc_q, sum_p, sum_q, own_p, own_q,
           in_sem, x_s, x_r, c_s, c_r, r1_s, r1_r, k_s, k_r, r2p_s, r2q_s, r2p_r, r2q_r,
           a1p_s, a1q_s, a1p_r, a1q_r, a2_s, a2_r, f_s, f_r):
    hist, x = lax.axis_index("hist"), lax.axis_index("col")
    core = hist % 2
    z, y = hist // 16, (hist // 2) % 8
    a = y * (1 - core) + z * core
    b = z * (1 - core) + y * core
    step_a, step_b = 2 + 14 * core, 16 - 14 * core
    base = COLS * core
    other = COLS * (1 - core)

    def at_a(pos):
        return (pos * step_a + b * step_b + core, x)

    def at_b(pos):
        return (a * step_a + pos * step_b + core, x)

    def at_x(pos):
        return (hist, pos)

    sibling = (hist + 1 - 2 * core, x)

    def remote(src, dst, send, recv, device):
        return pltpu.make_async_remote_copy(
            src_ref=src, dst_ref=dst, send_sem=send, recv_sem=recv, device_id=device, device_id_type=MESH
        )

    loads = [pltpu.make_async_copy(sr_ref, raw.at[0], in_sem.at[0]), pltpu.make_async_copy(sl_ref, raw.at[1], in_sem.at[1])]
    for half, first in ((0, other), (1, base)):
        for term, ref in ((0, gl_ref), (1, ga_ref)):
            columns = pl.ds(first, COLS)
            loads.append(pltpu.make_async_copy(ref.at[:, columns], green.at[term, :, columns], in_sem.at[2 + 2 * half + term]))
    for load in loads:
        load.start()

    barrier = pltpu.get_barrier_semaphore()

    def hail(device):
        pl.semaphore_signal(barrier, inc=1, device_id=device, device_id_type=MESH)

    hail(sibling)
    for j in (1, 2, 3):
        hail(at_x((x + j) % 4))

    def hail_rings(d, carry):
        hail(at_a((a + d) % RING))
        hail(at_b((b + d) % RING))
        return carry

    lax.fori_loop(1, RING, hail_rings, 0)

    loads[0].wait()
    loads[1].wait()
    low = lax.broadcasted_iota(jnp.int32, (16, 128), 1) < 64
    for term in range(2):
        for t in range(4):
            now = time_ref[t]
            for pair in range(2):
                v = []
                for k in range(2):
                    tb = 2 * pair + k
                    value = raw[term, t, tb].astype(jnp.float32)
                    v.append(jnp.where(hist * 4 + tb <= now, value, jnp.zeros_like(value)))
                depth = slice(128 * pair, 128 * pair + 128)
                re = jnp.where(low, v[0], pltpu.roll(v[1], 64, 1))
                im = jnp.where(low, pltpu.roll(v[0], 64, 1), v[1])
                left[term, 0, 16 * t : 16 * t + 16, depth] = re.astype(jnp.bfloat16)
                left[term, 0, 64 + 16 * t : 80 + 16 * t, depth] = im.astype(jnp.bfloat16)

    sign = jnp.where(lax.broadcasted_iota(jnp.int32, (64, 128), 1) < 64, -1.0, 1.0).astype(jnp.float32)

    def products(first_stage, n, first_col, target, masked):
        def two(j, carry):
            rights = []
            for term in range(2):
                columns = []
                for k in range(2):
                    c = first_col + 2 * j + k
                    rows = []
                    for tb in range(4):
                        g = green[term, tb, c]
                        if not masked:
                            g = jnp.where(hist * 4 + tb >= start_ref[c], g, jnp.zeros_like(g))
                            green[term, tb, c] = g
                        rows.append(g)
                    columns.append(jnp.concatenate(rows, axis=0))
                rights.append(jnp.concatenate(columns, axis=1))
            acc = None
            for term in range(2):
                lhs = left[term, first_stage : first_stage + n].reshape(n * 128, 256)
                d = jnp.dot(lhs, rights[term], preferred_element_type=jnp.float32)
                acc = d if acc is None else acc + d
            for i in range(n):
                for k in range(2):
                    one = acc[128 * i : 128 * i + 64, 128 * k : 128 * k + 128]
                    two_ = acc[128 * i + 64 : 128 * i + 128, 128 * k : 128 * k + 128]
                    value = one + pltpu.roll(two_, 64, 1) * sign
                    target[first_stage + i, 2 * j + k] = value.reshape(4, 16, 128)
            return carry

        lax.fori_loop(0, COLS // 2, two, 0)

    def pair_copy(s, n):
        at = pl.ds(s, n)
        return remote(c_send.at[at], c_recv.at[at], c_s.at[s], c_r.at[s], sibling)

    def encode(s):
        def add(c, most):
            v = part[s, c] + c_recv[s, c]
            part[s, c] = v
            return jnp.maximum(most, jnp.max(jnp.abs(v).reshape(8, 8, 128), axis=0))

        most = lax.fori_loop(0, COLS, add, jnp.zeros((8, 128), jnp.float32))
        most = jnp.maximum(jnp.max(most, axis=0, keepdims=True), 1e-33)
        scale[s] = most * (1.0 / 32767.0)
        factor = (32767.0 / most).reshape(1, 1, 128)

        def code(c, carry):
            coded[s, c] = jnp.round(part[s, c] * factor).astype(jnp.int32).astype(jnp.int16)
            return carry

        lax.fori_loop(0, COLS, code, 0)

    def ring_one(s):
        def send(d, carry):
            i = (a + d) % RING
            remote(coded.at[s, i], rx_p.at[s, d - 1], r1_s.at[s, 0], r1_r.at[s, 0], at_a(i)).start()
            remote(scale.at[s], sc_p.at[s, d - 1], k_s.at[s, 0], k_r.at[s, 0], at_a(i)).start()
            i = (b + d) % RING
            remote(coded.at[s, 8 + i // 2, pl.ds(2 * (i % 2), 2)], rx_q.at[s, d - 1], r1_s.at[s, 1], r1_r.at[s, 1], at_b(i)).start()
            remote(scale.at[s], sc_q.at[s, d - 1], k_s.at[s, 1], k_r.at[s, 1], at_b(i)).start()
            return carry

        lax.fori_loop(1, RING, send, 0)

    def ring_one_all(s):
        return [
            remote(rx_p.at[s], rx_p.at[s], r1_s.at[s, 0], r1_r.at[s, 0], sibling),
            remote(sc_p.at[s], sc_p.at[s], k_s.at[s, 0], k_r.at[s, 0], sibling),
            remote(rx_q.at[s], rx_q.at[s], r1_s.at[s, 1], r1_r.at[s, 1], sibling),
            remote(sc_q.at[s], sc_q.at[s], k_s.at[s, 1], k_r.at[s, 1], sibling),
        ]

    def p_copy(s, k):
        o = 4 * (s % 2) + k
        return o, remote(sum_p.at[s, k], own_p.at[s // 2, (b - o + RING) % RING - 1], r2p_s.at[s, k], r2p_r.at[s // 2], at_b(o))

    def q_copy(s, k):
        o = 2 * s + k
        return o, remote(sum_q.at[s, k], own_q.at[(a - o + RING) % RING - 1], r2q_s.at[s, k], r2q_r.at[0], at_a(o))

    def ring_two(s):
        for copy in ring_one_all(s):
            copy.wait_recv()
        total = part[s, a]
        for d in range(RING - 1):
            total = total + rx_p[s, d].astype(jnp.int32).astype(jnp.float32) * sc_p[s, d].reshape(1, 1, 128)
        sum_p[s] = total
        total = part[s, 8 + b // 2, pl.ds(2 * (b % 2), 2)]
        for d in range(RING - 1):
            total = total + rx_q[s, d].astype(jnp.int32).astype(jnp.float32) * sc_q[s, d].reshape(1, 1, 128)
        sum_q[s] = total
        for k in range(4):
            o, copy = p_copy(s, k)
            pl.when(o != b)(copy.start)
        for k in range(2):
            o, copy = q_copy(s, k)
            pl.when(o != a)(copy.start)

    def rows_of(s):
        return (x + STEP[s]) % 4

    def p_tile(s, k):
        return out_ref.at[k, base + a, rows_of(s)]

    def q_tile(s, k):
        return out_ref.at[2 * (b % 2) + k, base + 8 + b // 2, rows_of(s)]

    def own(s):
        @pl.when(b // 4 == s % 2)
        def _():
            u = s // 2
            remote(own_p.at[u], own_p.at[u], r2p_s.at[s, 0], r2p_r.at[u], sibling).wait_recv()
            total = sum_p[s, b % 4]
            for d in range(RING - 1):
                total = total + own_p[u, d]
            tile = p_tile(s, b % 4)
            tile[...] = total.astype(jnp.bfloat16)

            def send(d, carry):
                remote(tile, tile, a1p_s.at[u], a1p_r.at[s, b % 4], at_b((b + d) % RING)).start()
                return carry

            lax.fori_loop(1, RING, send, 0)

        @pl.when(a // 2 == s)
        def _():
            remote(own_q, own_q, r2q_s.at[s, 0], r2q_r.at[0], sibling).wait_recv()
            total = sum_q[s, a % 2]
            for d in range(RING - 1):
                total = total + own_q[d]
            tile = q_tile(s, a % 2)
            tile[...] = total.astype(jnp.bfloat16)

            def send(d, carry):
                remote(tile, tile, a1q_s.at[0], a1q_r.at[s, a % 2], at_a((a + d) % RING)).start()
                return carry

            lax.fori_loop(1, RING, send, 0)

    def spread(s):
        for k in range(4):
            tile = p_tile(s, k)
            copy = remote(tile, tile, a1p_s.at[0], a1p_r.at[s, k], sibling)
            pl.when(4 * (s % 2) + k != b)(copy.wait_recv)
        mine = out_ref.at[:, base + a, rows_of(s)]

        def send_p(d, carry):
            remote(mine, mine, a2_s.at[s, 0], a2_r.at[s, 0], at_a((a + d) % RING)).start()
            return carry

        lax.fori_loop(1, RING, send_p, 0)
        for k in range(2):
            tile = q_tile(s, k)
            copy = remote(tile, tile, a1q_s.at[0], a1q_r.at[s, k], sibling)
            pl.when(2 * s + k != a)(copy.wait_recv)
        my_q = out_ref.at[pl.ds(2 * (b % 2), 2), base + 8 + b // 2, rows_of(s)]

        def send_q(d, carry):
            remote(my_q, my_q, a2_s.at[s, 1], a2_r.at[s, 1], at_b((b + d) % RING)).start()
            return carry

        lax.fori_loop(1, RING, send_q, 0)

    def spread_all(s):
        p = out_ref.at[:, pl.ds(base, 7), rows_of(s)]
        q = out_ref.at[pl.ds(0, 2), pl.ds(base, 7), rows_of(s)]
        return [remote(p, p, a2_s.at[s, 0], a2_r.at[s, 0], sibling), remote(q, q, a2_s.at[s, 1], a2_r.at[s, 1], sibling)]

    def hand_over(s):
        mine = out_ref.at[:, pl.ds(base, COLS), rows_of(s)]
        return remote(mine, mine, f_s.at[s], f_r.at[s], sibling)

    def forward(s):
        for copy in spread_all(s):
            copy.wait_recv()
        hand_over(s).start()

    def quarter(stage):
        return remote(left.at[:, 0], left.at[:, stage], x_s.at[stage - 1], x_r.at[stage - 1], at_x((x + 4 - STEP[stage]) % 4))

    loads[2].wait()
    loads[3].wait()
    products(0, 1, other, c_send, False)
    pl.semaphore_wait(barrier, 18)
    for stage in (1, 2, 3):
        quarter(stage).start()
    pair_copy(0, 1).start()
    loads[4].wait()
    loads[5].wait()
    products(0, 1, base, part, False)
    pair_copy(0, 1).wait_recv()
    encode(0)
    ring_one(0)
    quarter(1).wait_recv()
    quarter(2).wait_recv()
    products(1, 2, other, c_send, True)
    pair_copy(1, 2).start()
    products(1, 2, base, part, True)
    pair_copy(1, 2).wait_recv()
    for s in (1, 2):
        encode(s)
        ring_one(s)
    ring_two(0)
    quarter(3).wait_recv()
    products(3, 1, other, c_send, True)
    pair_copy(3, 1).start()
    products(3, 1, base, part, True)
    pair_copy(3, 1).wait_recv()
    encode(3)
    ring_one(3)
    own(0)
    ring_two(1)
    ring_two(2)
    ring_two(3)
    spread(0)
    own(1)
    own(2)
    own(3)
    spread(1)
    forward(0)
    spread(2)
    spread(3)
    for s in (1, 2, 3):
        forward(s)
    for s in range(4):
        hand_over(s).wait_recv()

    for stage in (1, 2, 3):
        quarter(stage).wait_send()
    for s, n in ((0, 1), (1, 2), (3, 1)):
        pair_copy(s, n).wait_send()
    for s in range(4):
        for copy in ring_one_all(s):
            copy.wait_send()
        for k in range(4):
            o, copy = p_copy(s, k)
            pl.when(o != b)(copy.wait_send)
        for k in range(2):
            o, copy = q_copy(s, k)
            pl.when(o != a)(copy.wait_send)
        for copy in spread_all(s):
            copy.wait_send()
        hand_over(s).wait_send()
    seven = out_ref.at[0, pl.ds(0, 7), 0]
    for u in range(2):
        remote(seven, seven, a1p_s.at[u], a1p_r.at[0, 0], sibling).wait_send()
    remote(seven, seven, a1q_s.at[0], a1q_r.at[0, 0], sibling).wait_send()


def on_device(sigma_ret, sigma_less, green_less, green_adv, time_now, col_start):
    dma = pltpu.SemaphoreType.DMA
    f32, bf16, i16 = jnp.float32, jnp.bfloat16, jnp.int16
    out = pl.pallas_call(
        kernel,
        out_shape=jax.ShapeDtypeStruct((4, 24, 4, 16, 128), bf16),
        in_specs=[pl.BlockSpec(memory_space=pltpu.SMEM)] * 2 + [pl.BlockSpec(memory_space=pl.ANY)] * 4,
        out_specs=pl.BlockSpec(memory_space=pltpu.VMEM),
        scratch_shapes=[
            pltpu.VMEM((2, 4, 4, 16, 128), bf16),
            pltpu.VMEM((2, 4, 128, 256), bf16),
            pltpu.VMEM((2, 4, 24, 64, 128), bf16),
            pltpu.VMEM((4, COLS, 4, 16, 128), f32),
            pltpu.VMEM((4, COLS, 4, 16, 128), f32),
            pltpu.VMEM((4, COLS, 4, 16, 128), f32),
            pltpu.VMEM((4, COLS, 4, 16, 128), i16),
            pltpu.VMEM((4, 1, 128), f32),
            pltpu.VMEM((4, 7, 4, 16, 128), i16),
            pltpu.VMEM((4, 7, 2, 16, 128), i16),
            pltpu.VMEM((4, 7, 1, 128), f32),
            pltpu.VMEM((4, 7, 1, 128), f32),
            pltpu.VMEM((4, 4, 16, 128), f32),
            pltpu.VMEM((4, 2, 16, 128), f32),
            pltpu.VMEM((2, 7, 16, 128), f32),
            pltpu.VMEM((7, 16, 128), f32),
            dma((6,)),
            dma((3,)), dma((3,)),
            dma((4,)), dma((4,)),
            dma((4, 2)), dma((4, 2)),
            dma((4, 2)), dma((4, 2)),
            dma((4, 4)), dma((4, 2)), dma((2,)), dma((1,)),
            dma((2,)), dma((1,)), dma((4, 4)), dma((4, 2)),
            dma((4, 2)), dma((4, 2)),
            dma((4,)), dma((4,)),
        ],
        compiler_params=pltpu.CompilerParams(collective_id=0, has_side_effects=True, vmem_limit_bytes=40 * 1024 * 1024),
        cost_estimate=pl.CostEstimate(flops=1_610_612_736, bytes_accessed=5_000_000, transcendentals=0),
    )(time_now, col_start, sigma_ret, sigma_less, green_less, green_adv)
    return out.reshape(4, 24, 64, 128)


def solution(mesh):
    return jax.shard_map(
        on_device,
        mesh=mesh,
        in_specs=(
            P(None, "hist", "col", None),
            P(None, "hist", "col", None),
            P("hist", "col", None, None),
            P("hist", "col", None, None),
            P(),
            P("col"),
        ),
        out_specs=P(None, "col", None, None),
        check_vma=False,
    )
```

time: 570 us -> 64.5 us (0.11)
  blocking collectives: 548 us -> 0 us
  Pallas kernels: 0 us -> 57.2 us
  other arithmetic: 12.5 us -> 0 us
    psum x1 -> x0, blocking collectives: 528 us -> none  [on_device(): total = lax.psum(term, 'hist')]
    pallas_call x0 -> x1, Pallas kernels: none -> 57.2 us  [on_device(): pl.pallas_call(kernel, out_shape=jax.ShapeDtypeStruct((4, 24, 4, 16, 128)...]
    all_gather x2 -> x0, blocking collectives: 19.9 us -> none  [the longest x1 10.5 us: on_device(): lax.all_gather(sigma_less, 'col', axis=2, tiled=True)]
    neg x1 -> x0, other arithmetic: 6.97 us -> none  [widen(): lower = jnp.concatenate([-imag_part, real_part], axis=-1)]
    unnamed x12 -> x13, local copies, waits for them, and re-layouts: 0.02 us -> 6.95 us
where the time goes in v1:
time: 64.5 us; the launch traced here: 64.2 us
  Pallas kernels  57.2 us (89%)
  local copies, waits for them, and re-layouts  6.95 us (11%)
    pallas_call x1, Pallas kernels, on_device(): pl.pallas_call(kernel, out_shape=jax.ShapeDtypeStruct((4, 24, 4, 16, 128)...  57.2 us
    unnamed x13, local copies, waits for them, and re-layouts  6.95 us

profile of v1, /device:TPU:1, one launch (start us, length us, event | category | flops | bytes accessed | tf_op | source)
XLA Modules:
  0.0 64.2 jit_solution(18086757214412633717)
XLA Ops:
  0.0 0.0 copy-start
  0.0 1.4 %copy-done = bf16[4,24,64,128]{3,2,1,0:T(8,128)(2,1)S(1)} copy-done((bf16[4,24,64,128]{3,2,1,0:T(8,128)(2,1)S(1)}, bf16[4,24,64,128]{3,2,1,0:T(8,128)(2,1)}, u32[]{:S(2)}) %copy-start) | copy-done | bytes 1572888
  1.4 0.0 copy-start.1
  1.4 1.4 %copy-done.1 = bf16[4,24,64,128]{3,2,1,0:T(8,128)(2,1)S(1)} copy-done((bf16[4,24,64,128]{3,2,1,0:T(8,128)(2,1)S(1)}, bf16[4,24,64,128]{3,2,1,0:T(8,128)(2,1)}, u32[]{:S(2)}) %copy-start.1) | copy-done | bytes 1572888
  2.8 0.0 copy-start.2
  2.8 0.8 %copy-done.2 = bf16[4,4,16,128]{3,2,1,0:T(8,128)(2,1)S(1)} copy-done((bf16[4,4,16,128]{3,2,1,0:T(8,128)(2,1)S(1)}, bf16[4,4,16,128]{3,2,1,0:T(8,128)(2,1)}, u32[]{:S(2)}) %copy-start.2) | copy-done | bytes 65560
  3.7 0.0 copy-start.3
  3.7 0.8 %copy-done.3 = bf16[4,4,16,128]{3,2,1,0:T(8,128)(2,1)S(1)} copy-done((bf16[4,4,16,128]{3,2,1,0:T(8,128)(2,1)S(1)}, bf16[4,4,16,128]{3,2,1,0:T(8,128)(2,1)}, u32[]{:S(2)}) %copy-start.3) | copy-done | bytes 65560
  4.5 0.0 copy-start.4
  4.5 0.7 %copy-done.4 = s32[4]{0:T(128)S(1)} copy-done((s32[4]{0:T(128)S(1)}, s32[4]{0:T(128)}, u32[]{:S(2)}) %copy-start.4) | copy-done | bytes 40
  5.2 0.0 copy-start.5
  5.2 0.7 %copy-done.5 = s32[24]{0:T(128)S(1)} copy-done((s32[24]{0:T(128)S(1)}, s32[24]{0:T(128)}, u32[]{:S(2)}) %copy-start.5) | copy-done | bytes 120
  5.8 57.2 %shard_map.64 = bf16[4,24,4,16,128]{4,3,2,1,0:T(8,128)(2,1)S(1)} custom-call(s32[4]{0:T(128)S(1)} %copy-done.4, s32[24]{0:T(128)S(1)} %copy-done.5, bf16[4,4,16,128]{3,2,1,0:T(8,128)(2,1)S(1)} %copy-done.2, bf16[4,4,16,128]{3,2,1,0:T(8,128)(2,1)S(1)} %copy-done.3, bf16[4,24,64,128]{3,2,1,0:T(8,128)(2,1)S(1)} %copy-done, bf16[4,24,64,128]{3,2,1,0:T(8,128)(2,1)S(1)} %copy-done.1), custom_call_target="tpu_custom_call" | custom-call | flops 1610612736 | bytes 5000000 | tf_op jit(solution)/shard_map/pallas_call | solution.py:341
  63.1 1.1 %copy.8 = bf16[4,24,64,128]{3,2,1,0:T(8,128)(2,1)} copy(bf16[4,24,64,128]{3,2,1,0:T(8,128)(2,1)S(1)} %bitcast.1) | data formatting | bytes 3145728
Async XLA Ops:
  0.0 1.4 %copy-start = (bf16[4,24,64,128]{3,2,1,0:T(8,128)(2,1)S(1)}, bf16[4,24,64,128]{3,2,1,0:T(8,128)(2,1)}, u32[]{:S(2)}) copy-start(bf16[4,24,64,128]{3,2,1,0:T(8,128)(2,1)} %gl_ref.1) | copy-start | bytes 4718596
  1.4 1.4 %copy-start.1 = (bf16[4,24,64,128]{3,2,1,0:T(8,128)(2,1)S(1)}, bf16[4,24,64,128]{3,2,1,0:T(8,128)(2,1)}, u32[]{:S(2)}) copy-start(bf16[4,24,64,128]{3,2,1,0:T(8,128)(2,1)} %ga_ref.1) | copy-start | bytes 4718596
  2.8 0.8 %copy-start.2 = (bf16[4,4,16,128]{3,2,1,0:T(8,128)(2,1)S(1)}, bf16[4,4,16,128]{3,2,1,0:T(8,128)(2,1)}, u32[]{:S(2)}) copy-start(bf16[4,4,16,128]{3,2,1,0:T(8,128)(2,1)} %sr_ref.1) | copy-start | bytes 196612
  3.7 0.8 %copy-start.3 = (bf16[4,4,16,128]{3,2,1,0:T(8,128)(2,1)S(1)}, bf16[4,4,16,128]{3,2,1,0:T(8,128)(2,1)}, u32[]{:S(2)}) copy-start(bf16[4,4,16,128]{3,2,1,0:T(8,128)(2,1)} %sl_ref.1) | copy-start | bytes 196612
  4.5 0.7 %copy-start.4 = (s32[4]{0:T(128)S(1)}, s32[4]{0:T(128)}, u32[]{:S(2)}) copy-start(s32[4]{0:T(128)} %time_ref.1) | copy-start | bytes 52
  5.2 0.7 %copy-start.5 = (s32[24]{0:T(128)S(1)}, s32[24]{0:T(128)}, u32[]{:S(2)}) copy-start(s32[24]{0:T(128)} %start_ref.1) | copy-start | bytes 292

commit v2 on v1

v2 whole, which is shorter than its diff:
```python
import functools

import jax
import jax.numpy as jnp
from jax import lax
from jax.experimental import pallas as pl
from jax.experimental.pallas import tpu as pltpu
from jax.sharding import PartitionSpec as P

MESH = pl.DeviceIdType.MESH
RING = 8
COLS = 12
STEP = (0, 1, 3, 2)


def kernel(time_ref, start_ref, sr_ref, sl_ref, gl_ref, ga_ref, out_ref,
           times, starts, raw, left, green, out, c_send, c_recv, part, coded, scale, rx_p, rx_q, sc_p, sc_q, xp, xq, kp, kq,
           in_sem, x_s, x_r, c_s, c_r, r1_s, r1_r, k_s, k_r, r2_s, r2_r, k2_s, k2_r,
           a2_s, a2_r, f_s, f_r, l_s):
    hist, x = lax.axis_index("hist"), lax.axis_index("col")
    core = hist % 2
    z, y = hist // 16, (hist // 2) % 8
    a = y * (1 - core) + z * core
    b = z * (1 - core) + y * core
    step_a, step_b = 2 + 14 * core, 16 - 14 * core
    base = COLS * core
    other = COLS * (1 - core)

    def at_a(pos):
        return (pos * step_a + b * step_b + core, x)

    def at_b(pos):
        return (a * step_a + pos * step_b + core, x)

    def at_x(pos):
        return (hist, pos)

    sibling = (hist + 1 - 2 * core, x)

    def remote(src, dst, send, recv, device):
        return pltpu.make_async_remote_copy(
            src_ref=src, dst_ref=dst, send_sem=send, recv_sem=recv, device_id=device, device_id_type=MESH
        )

    small = [
        pltpu.make_async_copy(time_ref, times, in_sem.at[6]),
        pltpu.make_async_copy(start_ref, starts, in_sem.at[7]),
    ]
    loads = [pltpu.make_async_copy(sr_ref, raw.at[0], in_sem.at[0]), pltpu.make_async_copy(sl_ref, raw.at[1], in_sem.at[1])]
    for half, first in ((0, other), (1, base)):
        for term, ref in ((0, gl_ref), (1, ga_ref)):
            columns = pl.ds(first, COLS)
            loads.append(pltpu.make_async_copy(ref.at[:, columns], green.at[term, :, columns], in_sem.at[2 + 2 * half + term]))
    for load in loads[:2] + small + loads[2:]:
        load.start()

    barrier = pltpu.get_barrier_semaphore()

    def hail(device):
        pl.semaphore_signal(barrier, inc=1, device_id=device, device_id_type=MESH)

    hail(sibling)
    for j in (1, 2, 3):
        hail(at_x((x + j) % 4))

    def hail_rings(d, carry):
        hail(at_a((a + d) % RING))
        hail(at_b((b + d) % RING))
        return carry

    lax.fori_loop(1, RING, hail_rings, 0)

    for load in loads[:2] + small:
        load.wait()
    low = lax.broadcasted_iota(jnp.int32, (16, 128), 1) < 64
    for term in range(2):
        for t in range(4):
            now = times[t]
            for pair in range(2):
                v = []
                for k in range(2):
                    tb = 2 * pair + k
                    value = raw[term, t, tb].astype(jnp.float32)
                    v.append(jnp.where(hist * 4 + tb <= now, value, jnp.zeros_like(value)))
                depth = slice(128 * pair, 128 * pair + 128)
                re = jnp.where(low, v[0], pltpu.roll(v[1], 64, 1))
                im = jnp.where(low, pltpu.roll(v[0], 64, 1), v[1])
                left[term, 0, 16 * t : 16 * t + 16, depth] = re.astype(jnp.bfloat16)
                left[term, 0, 64 + 16 * t : 80 + 16 * t, depth] = im.astype(jnp.bfloat16)

    sign = jnp.where(lax.broadcasted_iota(jnp.int32, (64, 128), 1) < 64, -1.0, 1.0).astype(jnp.float32)

    def products(first_stage, n, first_col, target, masked):
        def two(j, carry):
            rights = []
            for term in range(2):
                columns = []
                for k in range(2):
                    c = first_col + 2 * j + k
                    rows = []
                    for tb in range(4):
                        g = green[term, tb, c]
                        if not masked:
                            g = jnp.where(hist * 4 + tb >= starts[c], g, jnp.zeros_like(g))
                            green[term, tb, c] = g
                        rows.append(g)
                    columns.append(jnp.concatenate(rows, axis=0))
                rights.append(jnp.concatenate(columns, axis=1))
            acc = None
            for term in range(2):
                lhs = left[term, first_stage : first_stage + n].reshape(n * 128, 256)
                d = jnp.dot(lhs, rights[term], preferred_element_type=jnp.float32)
                acc = d if acc is None else acc + d
            for i in range(n):
                for k in range(2):
                    one = acc[128 * i : 128 * i + 64, 128 * k : 128 * k + 128]
                    two_ = acc[128 * i + 64 : 128 * i + 128, 128 * k : 128 * k + 128]
                    value = one + pltpu.roll(two_, 64, 1) * sign
                    target[first_stage + i, 2 * j + k] = value.reshape(4, 16, 128)
            return carry

        lax.fori_loop(0, COLS // 2, two, 0, unroll=COLS // 2)

    def peers(send):
        def one(i, carry):
            send(4 + (i + 1) // 2 * (1 - 2 * (i % 2)))
            return carry

        lax.fori_loop(0, RING - 1, one, 0)

    def pair_copy(s, n):
        at = pl.ds(s, n)
        return remote(c_send.at[at], c_recv.at[at], c_s.at[s], c_r.at[s], sibling)

    def encode(s):
        def add(c, most):
            v = part[s, c] + c_recv[s, c]
            part[s, c] = v
            return jnp.maximum(most, jnp.max(jnp.abs(v).reshape(8, 8, 128), axis=0))

        most = lax.fori_loop(0, COLS, add, jnp.zeros((8, 128), jnp.float32))
        most = jnp.maximum(jnp.max(most, axis=0, keepdims=True), 1e-33)
        scale[s] = most * (1.0 / 32767.0)
        factor = (32767.0 / most).reshape(1, 1, 128)

        def code(c, carry):
            coded[s, c] = jnp.round(part[s, c] * factor).astype(jnp.int32).astype(jnp.int16)
            return carry

        lax.fori_loop(0, COLS, code, 0)

    def ring_one(s):
        def send(d):
            i = (a + d) % RING
            remote(coded.at[s, i], rx_p.at[s, d - 1], r1_s.at[s, 0], r1_r.at[s, 0], at_a(i)).start()
            remote(scale.at[s], sc_p.at[s, d - 1], k_s.at[s, 0], k_r.at[s, 0], at_a(i)).start()
            i = (b + d) % RING
            remote(coded.at[s, 8 + i // 2, pl.ds(2 * (i % 2), 2)], rx_q.at[s, d - 1], r1_s.at[s, 1], r1_r.at[s, 1], at_b(i)).start()
            remote(scale.at[s], sc_q.at[s, d - 1], k_s.at[s, 1], k_r.at[s, 1], at_b(i)).start()

        peers(send)

    def ring_one_all(s):
        return [
            remote(rx_p.at[s], rx_p.at[s], r1_s.at[s, 0], r1_r.at[s, 0], sibling),
            remote(sc_p.at[s], sc_p.at[s], k_s.at[s, 0], k_r.at[s, 0], sibling),
            remote(rx_q.at[s], rx_q.at[s], r1_s.at[s, 1], r1_r.at[s, 1], sibling),
            remote(sc_q.at[s], sc_q.at[s], k_s.at[s, 1], k_r.at[s, 1], sibling),
        ]

    def wide(codes, factor):
        return codes.astype(jnp.int32).astype(jnp.float32) * factor.reshape(1, 1, 128)

    def codes_of(total, codes, factor):
        most = jnp.max(jnp.abs(total).reshape(-1, 128), axis=0, keepdims=True)
        most = jnp.maximum(most, 1e-33)
        factor[...] = most * (1.0 / 32767.0)
        codes[...] = jnp.round(total * (32767.0 / most).reshape(1, 1, 128)).astype(jnp.int32).astype(jnp.int16)

    def ring_two(s):
        take(("one", s))
        total = part[s, a]
        for d in range(RING - 1):
            total = total + wide(rx_p[s, d], sc_p[s, d])
        codes_of(total, xp.at[s, b], kp.at[s, b])
        total = part[s, 8 + b // 2, pl.ds(2 * (b % 2), 2)]
        for d in range(RING - 1):
            total = total + wide(rx_q[s, d], sc_q[s, d])
        codes_of(total, xq.at[s, a], kq.at[s, a])

        def send(d):
            to = at_b((b + d) % RING)
            remote(xp.at[s, b], xp.at[s, b], r2_s.at[s, 0], r2_r.at[s, 0], to).start()
            remote(kp.at[s, b], kp.at[s, b], k2_s.at[s, 0], k2_r.at[s, 0], to).start()
            to = at_a((a + d) % RING)
            remote(xq.at[s, a], xq.at[s, a], r2_s.at[s, 1], r2_r.at[s, 1], to).start()
            remote(kq.at[s, a], kq.at[s, a], k2_s.at[s, 1], k2_r.at[s, 1], to).start()

        peers(send)
        copies = []
        for n, (codes, factors) in enumerate(((xp, kp), (xq, kq))):
            c, f = codes.at[s, pl.ds(0, 7)], factors.at[s, pl.ds(0, 7)]
            copies.append(remote(c, c, r2_s.at[s, n], r2_r.at[s, n], sibling))
            copies.append(remote(f, f, k2_s.at[s, n], k2_r.at[s, n], sibling))
        arrivals["two", s] = lambda: [copy.wait_recv() for copy in copies]
        departures.extend(copy.wait_send for copy in copies)

    def rows_of(s):
        return (x + STEP[s]) % 4

    def spread(s):
        take(("two", s))
        total = wide(xp[s, 0], kp[s, 0])
        for d in range(1, RING):
            total = total + wide(xp[s, d], kp[s, d])
        mine = out.at[:, a, rows_of(s)]
        mine[...] = total.astype(jnp.bfloat16)
        total = wide(xq[s, 0], kq[s, 0])
        for d in range(1, RING):
            total = total + wide(xq[s, d], kq[s, d])
        my_q = out.at[pl.ds(2 * (b % 2), 2), 8 + b // 2, rows_of(s)]
        my_q[...] = total.astype(jnp.bfloat16)

        def send(d):
            remote(mine, mine, a2_s.at[s, 0], a2_r.at[s, 0], at_a((a + d) % RING)).start()
            remote(my_q, my_q, a2_s.at[s, 1], a2_r.at[s, 1], at_b((b + d) % RING)).start()

        peers(send)
        arrivals["all", s] = lambda: [copy.wait_recv() for copy in spread_all(s)]
        departures.extend(copy.wait_send for copy in spread_all(s))

    def spread_all(s):
        p = out.at[:, pl.ds(0, 7), rows_of(s)]
        q = out.at[pl.ds(0, 2), pl.ds(0, 7), rows_of(s)]
        return [remote(p, p, a2_s.at[s, 0], a2_r.at[s, 0], sibling), remote(q, q, a2_s.at[s, 1], a2_r.at[s, 1], sibling)]

    def hand_over(s):
        mine = out.at[:, :, rows_of(s)]
        place = out_ref.at[:, pl.ds(base, COLS), rows_of(s)]
        return remote(mine, place, f_s.at[s], f_r.at[s], sibling), pltpu.make_async_copy(mine, place, l_s.at[s])

    def forward(s):
        take(("all", s))
        there, here = hand_over(s)
        there.start()
        here.start()
        arrivals["out", s] = there.wait_recv
        departures.append(there.wait_send)
        departures.append(here.wait)

    def quarter(stage):
        return remote(left.at[:, 0], left.at[:, stage], x_s.at[stage - 1], x_r.at[stage - 1], at_x((x + 4 - STEP[stage]) % 4))

    arrivals, departures = {}, []

    def take(key):
        arrivals.pop(key)()

    def start_quarter(stage):
        quarter(stage).start()
        arrivals["x", stage] = quarter(stage).wait_recv
        departures.append(quarter(stage).wait_send)

    def start_pair(s, n):
        pair_copy(s, n).start()
        arrivals["pair", s] = pair_copy(s, n).wait_recv
        departures.append(pair_copy(s, n).wait_send)

    def first_half():
        loads[2].wait()
        loads[3].wait()
        products(0, 1, other, c_send, False)

    def second_half():
        loads[4].wait()
        loads[5].wait()
        products(0, 1, base, part, False)

    def sums(s, n):
        take(("pair", s))
        for k in range(s, s + n):
            encode(k)
            ring_one(k)
            arrivals["one", k] = lambda k=k: [copy.wait_recv() for copy in ring_one_all(k)]
            departures.extend(copy.wait_send for copy in ring_one_all(k))

    steps = [
        first_half,
        lambda: pl.semaphore_wait(barrier, 18),
        lambda: (start_quarter(1), start_quarter(2)),
        lambda: start_pair(0, 1),
        second_half,
        lambda: start_quarter(3),
        lambda: sums(0, 1),
        lambda: (take(("x", 1)), take(("x", 2))),
        lambda: products(1, 2, other, c_send, True),
        lambda: start_pair(1, 2),
        lambda: products(1, 2, base, part, True),
        lambda: sums(1, 2),
        lambda: ring_two(0),
        lambda: take(("x", 3)),
        lambda: products(3, 1, other, c_send, True),
        lambda: start_pair(3, 1),
        lambda: products(3, 1, base, part, True),
        lambda: sums(3, 1),
        lambda: ring_two(1),
        lambda: spread(0),
        lambda: ring_two(2),
        lambda: ring_two(3),
        lambda: spread(1),
        lambda: forward(0),
        lambda: spread(2),
        lambda: spread(3),
        lambda: forward(1),
        lambda: forward(2),
        lambda: forward(3),
    ]
    for step in steps:
        step()
    for wait in list(arrivals.values()) + departures:
        wait()


def on_device(sigma_ret, sigma_less, green_less, green_adv, time_now, col_start):
    dma = pltpu.SemaphoreType.DMA
    f32, bf16, i16 = jnp.float32, jnp.bfloat16, jnp.int16
    out = pl.pallas_call(
        kernel,
        out_shape=jax.ShapeDtypeStruct((4, 24, 4, 16, 128), bf16),
        in_specs=[pl.BlockSpec(memory_space=pl.ANY)] * 6,
        out_specs=pl.BlockSpec(memory_space=pl.ANY),
        scratch_shapes=[
            pltpu.SMEM((4,), jnp.int32),
            pltpu.SMEM((24,), jnp.int32),
            pltpu.VMEM((2, 4, 4, 16, 128), bf16),
            pltpu.VMEM((2, 4, 128, 256), bf16),
            pltpu.VMEM((2, 4, 24, 64, 128), bf16),
            pltpu.VMEM((4, COLS, 4, 16, 128), bf16),
            pltpu.VMEM((4, COLS, 4, 16, 128), f32),
            pltpu.VMEM((4, COLS, 4, 16, 128), f32),
            pltpu.VMEM((4, COLS, 4, 16, 128), f32),
            pltpu.VMEM((4, COLS, 4, 16, 128), i16),
            pltpu.VMEM((4, 1, 128), f32),
            pltpu.VMEM((4, 7, 4, 16, 128), i16),
            pltpu.VMEM((4, 7, 2, 16, 128), i16),
            pltpu.VMEM((4, 7, 1, 128), f32),
            pltpu.VMEM((4, 7, 1, 128), f32),
            pltpu.VMEM((4, 8, 4, 16, 128), i16),
            pltpu.VMEM((4, 8, 2, 16, 128), i16),
            pltpu.VMEM((4, 8, 1, 128), f32),
            pltpu.VMEM((4, 8, 1, 128), f32),
            dma((8,)),
            dma((3,)), dma((3,)),
            dma((4,)), dma((4,)),
            dma((4, 2)), dma((4, 2)),
            dma((4, 2)), dma((4, 2)),
            dma((4, 2)), dma((4, 2)), dma((4, 2)), dma((4, 2)),
            dma((4, 2)), dma((4, 2)),
            dma((4,)), dma((4,)), dma((4,)),
        ],
        compiler_params=pltpu.CompilerParams(collective_id=0, has_side_effects=True, vmem_limit_bytes=61000 * 1024),
        cost_estimate=pl.CostEstimate(flops=1_610_612_736, bytes_accessed=5_000_000, transcendentals=0),
    )(time_now, col_start, sigma_ret, sigma_less, green_less, green_adv)
    return out.reshape(4, 24, 64, 128)


def solution(mesh):
    return jax.shard_map(
        on_device,
        mesh=mesh,
        in_specs=(
            P(None, "hist", "col", None),
            P(None, "hist", "col", None),
            P("hist", "col", None, None),
            P("hist", "col", None, None),
            P(),
            P("col"),
        ),
        out_specs=P(None, "col", None, None),
        check_vma=False,
    )
```

time: 64.5 us -> 55.3 us (0.86)
  Pallas kernels: 57.2 us -> 52.5 us
  local copies, waits for them, and re-layouts: 6.95 us -> 2.67 us
    pallas_call x1, Pallas kernels: 57.2 us -> 52.5 us  [on_device(): pl.pallas_call(kernel, out_shape=jax.ShapeDtypeStruct((4, 24, 4, 16, 128)...]
    unnamed x13 -> x1, local copies, waits for them, and re-layouts: 6.95 us -> 2.67 us
where the time goes in v2:
time: 55.3 us; the launch traced here: 55.2 us
  Pallas kernels  52.5 us (95%)
  local copies, waits for them, and re-layouts  2.67 us (5%)
    pallas_call x1, Pallas kernels, on_device(): pl.pallas_call(kernel, out_shape=jax.ShapeDtypeStruct((4, 24, 4, 16, 128)...  52.5 us
    unnamed x1, local copies, waits for them, and re-layouts  2.67 us

profile of v2, /device:TPU:1, one launch (start us, length us, event | category | flops | bytes accessed | tf_op | source)
XLA Modules:
  0.0 55.2 jit_solution(443720624597832042)
XLA Ops:
  0.0 52.5 %shard_map.64 = bf16[4,24,4,16,128]{4,3,2,1,0:T(8,128)(2,1)} custom-call(s32[4]{0:T(128)} %time_ref.1, s32[24]{0:T(128)} %start_ref.1, bf16[4,4,16,128]{3,2,1,0:T(8,128)(2,1)} %sr_ref.1, bf16[4,4,16,128]{3,2,1,0:T(8,128)(2,1)} %sl_ref.1, bf16[4,24,64,128]{3,2,1,0:T(8,128)(2,1)} %gl_ref.1, bf16[4,24,64,128]{3,2,1,0:T(8,128)(2,1)} %ga_ref.1), custom_call_target="tpu_custom_call" | custom-call | flops 1610612736 | bytes 5000000 | tf_op jit(solution)/shard_map/pallas_call | solution.py:327
  52.5 2.7 %copy.8 = bf16[4,24,64,128]{3,2,1,0:T(8,128)(2,1)} copy(bf16[4,24,64,128]{3,2,1,0:T(8,128)(2,1)} %bitcast.1) | data formatting | bytes 3145728

commit v3 on v2

v3 whole, which is shorter than its diff:
```python
import functools

import jax
import jax.numpy as jnp
from jax import lax
from jax.experimental import pallas as pl
from jax.experimental.pallas import tpu as pltpu
from jax.sharding import PartitionSpec as P

MESH = pl.DeviceIdType.MESH
RING = 8
PIECES = 4
COLS = 12
OWNED = (0, 1)


def kernel(time_ref, start_ref, sr_ref, sl_ref, gl_ref, ga_ref, out_ref,
           times, starts, raw, left, green, out, c_send, c_recv, part, coded, scale, rx_p, rx_q, sc_p, sc_q, sum_p, sum_q, own_p, own_q, xp, xq, kp, kq,
           in_sem, x_s, x_r, c_s, c_r, r1_s, r1_r, k_s, k_r, r2p_s, r2q_s, r2p_r, r2q_r, r2_s, r2_r, k2_s, k2_r,
           a1p_s, a1q_s, a1p_r, a1q_r, a2_s, a2_r, f_s, f_r, l_s):
    hist, x = lax.axis_index("hist"), lax.axis_index("col")
    core = hist % 2
    z, y = hist // 16, (hist // 2) % 8
    a = y * (1 - core) + z * core
    b = z * (1 - core) + y * core
    step_a, step_b = 2 + 14 * core, 16 - 14 * core
    base = COLS * core
    other = COLS * (1 - core)

    peers_a, peers_b = [], []
    for d in (4, 3, 5, 2, 6, 1, 7):
        pos = lax.rem(a + d, RING)
        peers_a.append((d, pos, (pos * step_a + b * step_b + core, x)))
        pos = lax.rem(b + d, RING)
        peers_b.append((d, pos, (a * step_a + pos * step_b + core, x)))

    def at_x(pos):
        return (hist, pos)

    sibling = (hist + 1 - 2 * core, x)

    def remote(src, dst, send, recv, device):
        return pltpu.make_async_remote_copy(
            src_ref=src, dst_ref=dst, send_sem=send, recv_sem=recv, device_id=device, device_id_type=MESH
        )

    barrier = pltpu.get_barrier_semaphore()
    for device in [d[2] for pair in zip(peers_a, peers_b) for d in pair] + [at_x(lax.rem(x + j, 4)) for j in (2, 1, 3)] + [sibling]:
        pl.semaphore_signal(barrier, inc=1, device_id=device, device_id_type=MESH)

    small = [
        pltpu.make_async_copy(time_ref, times, in_sem.at[6]),
        pltpu.make_async_copy(start_ref, starts, in_sem.at[7]),
    ]
    loads = [pltpu.make_async_copy(sr_ref, raw.at[0], in_sem.at[0]), pltpu.make_async_copy(sl_ref, raw.at[1], in_sem.at[1])]
    for half, first in ((0, other), (1, base)):
        for term, ref in ((0, gl_ref), (1, ga_ref)):
            columns = pl.ds(first, COLS)
            loads.append(pltpu.make_async_copy(ref.at[:, columns], green.at[term, :, columns], in_sem.at[2 + 2 * half + term]))
    for load in loads[:2] + small + loads[2:]:
        load.start()

    for load in loads[:2] + small:
        load.wait()
    low = lax.broadcasted_iota(jnp.int32, (16, 128), 1) < 64
    for term in range(2):
        for t in range(4):
            now = times[t]
            for pair in range(2):
                v = []
                for k in range(2):
                    tb = 2 * pair + k
                    value = raw[term, t, tb].astype(jnp.float32)
                    v.append(jnp.where(hist * 4 + tb <= now, value, jnp.zeros_like(value)))
                depth = slice(128 * pair, 128 * pair + 128)
                re = jnp.where(low, v[0], pltpu.roll(v[1], 64, 1))
                im = jnp.where(low, pltpu.roll(v[0], 64, 1), v[1])
                left[0, term, 0, t, :, depth] = re.astype(jnp.bfloat16)
                left[0, term, 1, t, :, depth] = im.astype(jnp.bfloat16)

    sign = jnp.where(lax.broadcasted_iota(jnp.int32, (64, 128), 1) < 64, -1.0, 1.0).astype(jnp.float32)

    def products(stage, first_col, target, masked):
        def two(j, carry):
            rights = []
            for term in range(2):
                columns = []
                for k in range(2):
                    c = first_col + 2 * j + k
                    rows = []
                    for tb in range(4):
                        g = green[term, tb, c]
                        if not masked:
                            g = jnp.where(hist * 4 + tb >= starts[c], g, jnp.zeros_like(g))
                            green[term, tb, c] = g
                        rows.append(g)
                    columns.append(jnp.concatenate(rows, axis=0))
                rights.append(jnp.concatenate(columns, axis=1))
            acc = None
            for term in range(2):
                lhs = left[stage, term].reshape(128, 256)
                d = jnp.dot(lhs, rights[term], preferred_element_type=jnp.float32)
                acc = d if acc is None else acc + d
            for k in range(2):
                lanes = slice(128 * k, 128 * k + 128)
                value = acc[:64, lanes] + pltpu.roll(acc[64:, lanes], 64, 1) * sign
                target[2 * j + k, stage] = value.reshape(4, 16, 128)
            return carry

        lax.fori_loop(0, COLS // 2, two, 0, unroll=COLS // 2)

    def pair_copy(s):
        return remote(c_send.at[:, s], c_recv.at[:, s], c_s.at[s], c_r.at[s], sibling)

    def encode(s):
        def add(c, most):
            v = part[c, s] + c_recv[c, s]
            part[c, s] = v
            return jnp.maximum(most, jnp.max(jnp.abs(v).reshape(8, 8, 128), axis=0))

        most = lax.fori_loop(0, COLS, add, jnp.zeros((8, 128), jnp.float32), unroll=2)
        most = jnp.maximum(jnp.max(most, axis=0, keepdims=True), 1e-33)
        scale[s] = most * (1.0 / 32767.0)
        factor = (32767.0 / most).reshape(1, 1, 128)

        def code(c, carry):
            coded[c, s] = jnp.round(part[c, s] * factor).astype(jnp.int32).astype(jnp.int16)
            return carry

        lax.fori_loop(0, COLS, code, 0, unroll=2)

    def ring_one(s):
        for (d, i, to_a), (_, k, to_b) in zip(peers_a, peers_b):
            remote(coded.at[i, s], rx_p.at[s, d - 1], r1_s.at[s, 0], r1_r.at[s, 0], to_a).start()
            mine = coded.at[8 + k // 2, s, pl.ds(2 * (k % 2), 2)]
            remote(mine, rx_q.at[s, d - 1], r1_s.at[s, 1], r1_r.at[s, 1], to_b).start()
            remote(scale.at[s], sc_p.at[s, d - 1], k_s.at[s, 0], k_r.at[s, 0], to_a).start()
            remote(scale.at[s], sc_q.at[s, d - 1], k_s.at[s, 1], k_r.at[s, 1], to_b).start()
        copies = [
            remote(rx_p.at[s], rx_p.at[s], r1_s.at[s, 0], r1_r.at[s, 0], sibling),
            remote(sc_p.at[s], sc_p.at[s], k_s.at[s, 0], k_r.at[s, 0], sibling),
            remote(rx_q.at[s], rx_q.at[s], r1_s.at[s, 1], r1_r.at[s, 1], sibling),
            remote(sc_q.at[s], sc_q.at[s], k_s.at[s, 1], k_r.at[s, 1], sibling),
        ]
        arrivals["one", s] = lambda: [copy.wait_recv() for copy in copies]
        departures.extend(copy.wait_send for copy in copies)

    def wide(codes, factor):
        return codes.astype(jnp.int32).astype(jnp.float32) * factor.reshape(1, 1, 128)

    def codes_of(total, codes, factor):
        most = jnp.max(jnp.abs(total).reshape(-1, 128), axis=0, keepdims=True)
        most = jnp.maximum(most, 1e-33)
        factor[...] = most * (1.0 / 32767.0)
        codes[...] = jnp.round(total * (32767.0 / most).reshape(1, 1, 128)).astype(jnp.int32).astype(jnp.int16)

    def ring_one_sums(s):
        take(("one", s))
        total_p = part[a, s]
        for d in range(RING - 1):
            total_p = total_p + wide(rx_p[s, d], sc_p[s, d])
        total_q = part[8 + b // 2, s, pl.ds(2 * (b % 2), 2)]
        for d in range(RING - 1):
            total_q = total_q + wide(rx_q[s, d], sc_q[s, d])
        return total_p, total_q

    def tile_p(s, k):
        return out.at[a, s, k]

    def tile_q(s, k):
        return out.at[8 + b // 2, s, 2 * (b % 2) + k]

    def to_owners(s):
        sum_p[s], sum_q[s] = ring_one_sums(s)
        u = s // 2
        for k in range(4):
            o = 4 * (s % 2) + k
            to = (a * step_a + o * step_b + core, x)
            copy = remote(sum_p.at[s, k], own_p.at[u, lax.rem(b - o + 15, RING)], r2p_s.at[s, k], r2p_r.at[u], to)
            pl.when(o != b)(copy.start)
            departures.append(functools.partial(pl.when(o != b), copy.wait_send))
        for k in range(2):
            o = 2 * s + k
            to = (o * step_a + b * step_b + core, x)
            copy = remote(sum_q.at[s, k], own_q.at[lax.rem(a - o + 15, RING)], r2q_s.at[s, k], r2q_r.at[0], to)
            pl.when(o != a)(copy.start)
            departures.append(functools.partial(pl.when(o != a), copy.wait_send))
        all_p = remote(own_p.at[u, pl.ds(0, 7)], own_p.at[u, pl.ds(0, 7)], r2p_s.at[s, 0], r2p_r.at[u], sibling)
        all_q = remote(own_q.at[pl.ds(0, 7)], own_q.at[pl.ds(0, 7)], r2q_s.at[s, 0], r2q_r.at[0], sibling)
        arrivals["p", s] = lambda: pl.when(b // 4 == s % 2)(all_p.wait_recv)
        arrivals["q", s] = lambda: pl.when(a // 2 == s)(all_q.wait_recv)

    def own(s):
        u = s // 2
        take(("p", s))

        @pl.when(b // 4 == s % 2)
        def _():
            total = sum_p[s, b % 4]
            for d in range(RING - 1):
                total = total + own_p[u, d]
            tile = tile_p(s, b % 4)
            tile[...] = total.astype(jnp.bfloat16)
            for _, _, to_b in peers_b:
                remote(tile, tile, a1p_s.at[u], a1p_r.at[s, b % 4], to_b).start()

        take(("q", s))

        @pl.when(a // 2 == s)
        def _():
            total = sum_q[s, a % 2]
            for d in range(RING - 1):
                total = total + own_q[d]
            tile = tile_q(s, a % 2)
            tile[...] = total.astype(jnp.bfloat16)
            for _, _, to_a in peers_a:
                remote(tile, tile, a1q_s.at[0], a1q_r.at[s, a % 2], to_a).start()

        seven = out.at[pl.ds(0, 7), 0, 0]
        sent_p = remote(seven, seven, a1p_s.at[u], a1p_r.at[s, 0], sibling)
        sent_q = remote(seven, seven, a1q_s.at[0], a1q_r.at[s, 0], sibling)
        departures.append(functools.partial(pl.when(b // 4 == s % 2), sent_p.wait_send))
        departures.append(functools.partial(pl.when(a // 2 == s), sent_q.wait_send))
        for k in range(4):
            copy = remote(tile_p(s, k), tile_p(s, k), a1p_s.at[0], a1p_r.at[s, k], sibling)
            arrivals["tp", s, k] = functools.partial(pl.when(4 * (s % 2) + k != b), copy.wait_recv)
        for k in range(2):
            copy = remote(tile_q(s, k), tile_q(s, k), a1q_s.at[0], a1q_r.at[s, k], sibling)
            arrivals["tq", s, k] = functools.partial(pl.when(2 * s + k != a), copy.wait_recv)

    def to_all(s):
        total_p, total_q = ring_one_sums(s)
        my_p, my_kp = xp.at[s, b], kp.at[s, b]
        codes_of(total_p, my_p, my_kp)
        my_q, my_kq = xq.at[s, a], kq.at[s, a]
        codes_of(total_q, my_q, my_kq)
        for (_, _, to_a), (_, _, to_b) in zip(peers_a, peers_b):
            remote(my_p, my_p, r2_s.at[s, 0], r2_r.at[s, 0], to_b).start()
            remote(my_q, my_q, r2_s.at[s, 1], r2_r.at[s, 1], to_a).start()
            remote(my_kp, my_kp, k2_s.at[s, 0], k2_r.at[s, 0], to_b).start()
            remote(my_kq, my_kq, k2_s.at[s, 1], k2_r.at[s, 1], to_a).start()
        copies = []
        for m, (codes, factors) in enumerate(((xp, kp), (xq, kq))):
            c, f = codes.at[s, pl.ds(0, 7)], factors.at[s, pl.ds(0, 7)]
            copies.append(remote(c, c, r2_s.at[s, m], r2_r.at[s, m], sibling))
            copies.append(remote(f, f, k2_s.at[s, m], k2_r.at[s, m], sibling))
        arrivals["two", s] = lambda: [copy.wait_recv() for copy in copies]
        departures.extend(copy.wait_send for copy in copies)

    def add_all(s):
        take(("two", s))
        total = wide(xp[s, 0], kp[s, 0])
        for d in range(1, RING):
            total = total + wide(xp[s, d], kp[s, d])
        out[a, s] = total.astype(jnp.bfloat16)
        total = wide(xq[s, 0], kq[s, 0])
        for d in range(1, RING):
            total = total + wide(xq[s, d], kq[s, d])
        out[8 + b // 2, s, pl.ds(2 * (b % 2), 2)] = total.astype(jnp.bfloat16)

    def ring_two(s):
        (to_owners if s in OWNED else to_all)(s)

    def spread(s):
        if s in OWNED:
            for k in range(4):
                take(("tp", s, k))
            for k in range(2):
                take(("tq", s, k))
        else:
            add_all(s)
        mine, my_q = out.at[a, s], out.at[8 + b // 2, s, pl.ds(2 * (b % 2), 2)]
        for (_, _, to_a), (_, _, to_b) in zip(peers_a, peers_b):
            remote(mine, mine, a2_s.at[s, 0], a2_r.at[s, 0], to_a).start()
            remote(my_q, my_q, a2_s.at[s, 1], a2_r.at[s, 1], to_b).start()
        seven_p, seven_q = out.at[pl.ds(0, 7), s], out.at[pl.ds(0, 7), s, pl.ds(0, 2)]
        copies = [
            remote(seven_p, seven_p, a2_s.at[s, 0], a2_r.at[s, 0], sibling),
            remote(seven_q, seven_q, a2_s.at[s, 1], a2_r.at[s, 1], sibling),
        ]
        arrivals["all", s] = lambda: [copy.wait_recv() for copy in copies]
        departures.extend(copy.wait_send for copy in copies)

    def forward(s):
        take(("all", s))
        for k in range(4):
            if s in (0, 3):
                t, quarter = k, x + 2 * (s // 3)
            else:
                t, quarter = 2 * (s - 1) + k % 2, x + 1 + 2 * (k // 2)
            mine = out.at[:, s, k]
            place = out_ref.at[t, pl.ds(base, COLS), lax.rem(quarter, 4)]
            there = remote(mine, place, f_s.at[s, k], f_r.at[s, k], sibling)
            here = pltpu.make_async_copy(mine, place, l_s.at[s, k])
            there.start()
            here.start()
            arrivals["out", s, k] = there.wait_recv
            departures.append(there.wait_send)
            departures.append(here.wait)

    def gather(s):
        if s == 3:
            copies = [remote(left.at[0], left.at[3], x_s.at[4], x_r.at[4], at_x(lax.rem(x + 2, 4)))]
        else:
            copies = []
            for m, ahead in enumerate((3, 1)):
                src = left.at[0, :, :, pl.ds(2 * (s - 1), 2)]
                dst = left.at[s, :, :, pl.ds(2 * m, 2)]
                n = 2 * (s - 1) + m
                copies.append(remote(src, dst, x_s.at[n], x_r.at[n], at_x(lax.rem(x + ahead, 4))))
        for copy in copies:
            copy.start()
        arrivals["x", s] = lambda: [copy.wait_recv() for copy in copies]
        departures.extend(copy.wait_send for copy in copies)

    arrivals, departures = {}, []

    def take(key):
        arrivals.pop(key)()

    def half_one(s):
        if s == 0:
            pl.semaphore_wait(barrier, 18)
            gather(1)
            loads[2].wait()
            loads[3].wait()
        else:
            take(("x", s))
        products(s, other, c_send, s > 0)
        copy = pair_copy(s)
        copy.start()
        arrivals["pair", s] = copy.wait_recv
        departures.append(copy.wait_send)

    def half_two(s):
        if s == 0:
            loads[4].wait()
            loads[5].wait()
        products(s, base, part, s > 0)

    def sums(s):
        take(("pair", s))
        encode(s)
        ring_one(s)

    steps = [
        (half_one, 0), (gather, 2), (half_two, 0), (sums, 0), (gather, 3),
        (half_one, 1), (half_two, 1), (half_one, 2), (sums, 1), (half_two, 2), (sums, 2),
        (ring_two, 0),
        (half_one, 3), (half_two, 3), (sums, 3),
        (ring_two, 1), (own, 0), (ring_two, 2), (ring_two, 3), (own, 1), (spread, 2), (spread, 0), (spread, 3), (spread, 1), (forward, 0), (forward, 2), (forward, 3), (forward, 1),
    ]
    steps = [(step, s) for step, s in steps if step is not own or s in OWNED]
    for step, s in steps:
        step(s)
    for wait in list(arrivals.values()) + departures:
        wait()


def deliver(src, dst, held, arrive, leave):
    each = 4 * 24 // PIECES
    inward, outward = [], []
    for k in range(PIECES):
        at = (k * each // 24, pl.ds(k * each % 24, each))
        inward.append(pltpu.make_async_copy(src.at[at], held.at[at], arrive.at[k]))
        outward.append(pltpu.make_async_copy(held.at[at], dst.at[at], leave.at[k]))
    for copy in inward:
        copy.start()
    for a, b in zip(inward, outward):
        a.wait()
        b.start()
    for copy in outward:
        copy.wait()


def on_device(sigma_ret, sigma_less, green_less, green_adv, time_now, col_start):
    dma = pltpu.SemaphoreType.DMA
    f32, bf16, i16 = jnp.float32, jnp.bfloat16, jnp.int16
    out = pl.pallas_call(
        kernel,
        out_shape=jax.ShapeDtypeStruct((4, 24, 4, 16, 128), bf16),
        in_specs=[pl.BlockSpec(memory_space=pl.ANY)] * 6,
        out_specs=pl.BlockSpec(memory_space=pl.ANY),
        scratch_shapes=[
            pltpu.SMEM((4,), jnp.int32),
            pltpu.SMEM((24,), jnp.int32),
            pltpu.VMEM((2, 4, 4, 16, 128), bf16),
            pltpu.VMEM((4, 2, 2, 4, 16, 256), bf16),
            pltpu.VMEM((2, 4, 24, 64, 128), bf16),
            pltpu.VMEM((COLS, 4, 4, 16, 128), bf16),
            pltpu.VMEM((COLS, 4, 4, 16, 128), f32),
            pltpu.VMEM((COLS, 4, 4, 16, 128), f32),
            pltpu.VMEM((COLS, 4, 4, 16, 128), f32),
            pltpu.VMEM((COLS, 4, 4, 16, 128), i16),
            pltpu.VMEM((4, 1, 128), f32),
            pltpu.VMEM((4, 7, 4, 16, 128), i16),
            pltpu.VMEM((4, 7, 2, 16, 128), i16),
            pltpu.VMEM((4, 7, 1, 128), f32),
            pltpu.VMEM((4, 7, 1, 128), f32),
            pltpu.VMEM((4, 4, 16, 128), f32),
            pltpu.VMEM((4, 2, 16, 128), f32),
            pltpu.VMEM((2, 8, 16, 128), f32),
            pltpu.VMEM((8, 16, 128), f32),
            pltpu.VMEM((4, 8, 4, 16, 128), i16),
            pltpu.VMEM((4, 8, 2, 16, 128), i16),
            pltpu.VMEM((4, 8, 1, 128), f32),
            pltpu.VMEM((4, 8, 1, 128), f32),
            dma((8,)),
            dma((5,)), dma((5,)),
            dma((4,)), dma((4,)),
            dma((4, 2)), dma((4, 2)),
            dma((4, 2)), dma((4, 2)),
            dma((4, 4)), dma((4, 2)), dma((2,)), dma((1,)),
            dma((4, 2)), dma((4, 2)), dma((4, 2)), dma((4, 2)),
            dma((2,)), dma((1,)), dma((4, 4)), dma((4, 2)),
            dma((4, 2)), dma((4, 2)),
            dma((4, 4)), dma((4, 4)), dma((4, 4)),
        ],
        compiler_params=pltpu.CompilerParams(collective_id=0, has_side_effects=True, vmem_limit_bytes=61000 * 1024),
        cost_estimate=pl.CostEstimate(flops=1_610_612_736, bytes_accessed=5_000_000, transcendentals=0),
    )(time_now, col_start, sigma_ret, sigma_less, green_less, green_adv)
    out = out.reshape(4, 24, 64, 128)
    return pl.pallas_call(
        deliver,
        out_shape=jax.ShapeDtypeStruct(out.shape, out.dtype),
        in_specs=[pl.BlockSpec(memory_space=pl.ANY)],
        out_specs=pl.BlockSpec(memory_space=pl.ANY),
        scratch_shapes=[pltpu.VMEM(out.shape, out.dtype), dma((PIECES,)), dma((PIECES,))],
        compiler_params=pltpu.CompilerParams(vmem_limit_bytes=61000 * 1024),
        cost_estimate=pl.CostEstimate(flops=0, bytes_accessed=3_145_728, transcendentals=0),
    )(out)


def solution(mesh):
    return jax.shard_map(
        on_device,
        mesh=mesh,
        in_specs=(
            P(None, "hist", "col", None),
            P(None, "hist", "col", None),
            P("hist", "col", None, None),
            P("hist", "col", None, None),
            P(),
            P("col"),
        ),
        out_specs=P(None, "col", None, None),
        check_vma=False,
    )
```

time: 55.3 us -> 53.9 us (0.975)
  local copies, waits for them, and re-layouts: 2.67 us -> 0 us
  Pallas kernels: 52.5 us -> 53.7 us
    unnamed x1 -> x0, local copies, waits for them, and re-layouts: 2.67 us -> none
    pallas_call x0 -> x1, Pallas kernels: none -> 2.2 us  [on_device(): pl.pallas_call(deliver, out_shape=jax.ShapeDtypeStruct(out.shape, out.dty...]
    pallas_call x1, Pallas kernels: 52.5 us -> 51.5 us  [on_device(): pl.pallas_call(kernel, out_shape=jax.ShapeDtypeStruct((4, 24, 4, 16, 128)...]
where the time goes in v3:
time: 53.9 us; the launch traced here: 53.7 us
  Pallas kernels  53.7 us (100%)
    pallas_call x1, Pallas kernels, on_device(): pl.pallas_call(kernel, out_shape=jax.ShapeDtypeStruct((4, 24, 4, 16, 128)...  51.5 us
    pallas_call x1, Pallas kernels, on_device(): pl.pallas_call(deliver, out_shape=jax.ShapeDtypeStruct(out.shape, out.dty...  2.2 us

profile of v3, /device:TPU:1, one launch (start us, length us, event | category | flops | bytes accessed | tf_op | source)
XLA Modules:
  0.0 53.7 jit_solution(160855600615037884)
XLA Ops:
  0.0 51.5 %shard_map.64 = bf16[4,24,4,16,128]{4,3,2,1,0:T(8,128)(2,1)} custom-call(s32[4]{0:T(128)} %time_ref.1, s32[24]{0:T(128)} %start_ref.1, bf16[4,4,16,128]{3,2,1,0:T(8,128)(2,1)} %sr_ref.1, bf16[4,4,16,128]{3,2,1,0:T(8,128)(2,1)} %sl_ref.1, bf16[4,24,64,128]{3,2,1,0:T(8,128)(2,1)} %gl_ref.1, bf16[4,24,64,128]{3,2,1,0:T(8,128)(2,1)} %ga_ref.1), custom_call_target="tpu_custom_call" | custom-call | flops 1610612736 | bytes 5000000 | tf_op jit(solution)/shard_map/pallas_call | solution.py:379
  51.5 2.2 %shard_map.65 = bf16[4,24,64,128]{3,2,1,0:T(8,128)(2,1)} custom-call(bf16[4,24,64,128]{3,2,1,0:T(8,128)(2,1)} %bitcast.1), custom_call_target="tpu_custom_call" | custom-call | bytes 3145728 | tf_op jit(solution)/shard_map/pallas_call | solution.py:423

commit v4 on v3

--- a/solution.py
+++ b/solution.py
@@ -11,7 +11,7 @@
 RING = 8
 PIECES = 4
 COLS = 12
-OWNED = (0, 1)
+OWNED = (0,)
 
 
 def kernel(time_ref, start_ref, sr_ref, sl_ref, gl_ref, ga_ref, out_ref,
@@ -344,11 +344,11 @@
         ring_one(s)
 
     steps = [
-        (half_one, 0), (gather, 2), (half_two, 0), (sums, 0), (gather, 3),
-        (half_one, 1), (half_two, 1), (half_one, 2), (sums, 1), (half_two, 2), (sums, 2),
+        (half_one, 0), (gather, 2), (half_two, 0), (sums, 0),
+        (half_one, 1), (gather, 3), (half_two, 1), (half_one, 2), (sums, 1), (half_two, 2), (sums, 2),
         (ring_two, 0),
         (half_one, 3), (half_two, 3), (sums, 3),
-        (ring_two, 1), (own, 0), (ring_two, 2), (ring_two, 3), (own, 1), (spread, 2), (spread, 0), (spread, 3), (spread, 1), (forward, 0), (forward, 2), (forward, 3), (forward, 1),
+        (ring_two, 1), (own, 0), (ring_two, 2), (ring_two, 3), (spread, 1), (spread, 0), (spread, 2), (spread, 3), (forward, 1), (forward, 0), (forward, 2), (forward, 3),
     ]
     steps = [(step, s) for step, s in steps if step is not own or s in OWNED]
     for step, s in steps:

time: 53.9 us -> 53.1 us (0.985)
  Pallas kernels: 53.7 us -> 53 us
    pallas_call x1, Pallas kernels: 51.5 us -> 50.8 us  [on_device(): pl.pallas_call(kernel, out_shape=jax.ShapeDtypeStruct((4, 24, 4, 16, 128)...]
where the time goes in v4:
time: 53.1 us; the launch traced here: 53 us
  Pallas kernels  53 us (100%)
    pallas_call x1, Pallas kernels, on_device(): pl.pallas_call(kernel, out_shape=jax.ShapeDtypeStruct((4, 24, 4, 16, 128)...  50.8 us
    pallas_call x1, Pallas kernels, on_device(): pl.pallas_call(deliver, out_shape=jax.ShapeDtypeStruct(out.shape, out.dty...  2.2 us

profile of v4, /device:TPU:1, one launch (start us, length us, event | category | flops | bytes accessed | tf_op | source)
XLA Modules:
  0.0 53.0 jit_solution(645252705858168822)
XLA Ops:
  0.0 50.8 %shard_map.64 = bf16[4,24,4,16,128]{4,3,2,1,0:T(8,128)(2,1)} custom-call(s32[4]{0:T(128)} %time_ref.1, s32[24]{0:T(128)} %start_ref.1, bf16[4,4,16,128]{3,2,1,0:T(8,128)(2,1)} %sr_ref.1, bf16[4,4,16,128]{3,2,1,0:T(8,128)(2,1)} %sl_ref.1, bf16[4,24,64,128]{3,2,1,0:T(8,128)(2,1)} %gl_ref.1, bf16[4,24,64,128]{3,2,1,0:T(8,128)(2,1)} %ga_ref.1), custom_call_target="tpu_custom_call" | custom-call | flops 1610612736 | bytes 5000000 | tf_op jit(solution)/shard_map/pallas_call | solution.py:379
  50.8 2.2 %shard_map.65 = bf16[4,24,64,128]{3,2,1,0:T(8,128)(2,1)} custom-call(bf16[4,24,64,128]{3,2,1,0:T(8,128)(2,1)} %bitcast.1), custom_call_target="tpu_custom_call" | custom-call | bytes 3145728 | tf_op jit(solution)/shard_map/pallas_call | solution.py:423
